TPU v7x, 32 devices: a whole 2x2x4 slice. The times are simulated.
32 devices in a mesh: seq: 16 (over z, x, core), fsdp: 2 (over y).
Axes of the slice: x: 2, y: 2, z: 4, core: 2. Of those that a mesh axis runs over, the one named last changes fastest.
Arguments:
- queries: bfloat16 [8192, 2048], P('seq', 'fsdp'), may hold values from -6 to 6
- keys: bfloat16 [8192, 2048], P('seq', 'fsdp'), may hold values from -6 to 6
- values: bfloat16 [8192, 2048], P('seq', 'fsdp'), may hold values from -6 to 6
- feature_weight: bfloat16 [16, 128, 128], P(None, 'fsdp', 'seq'), may hold values from -0.5 to 0.5
- norm_gain: bfloat16 [16, 128], P('fsdp'), may hold values from 0.099609375 to 1.8984375
- doc_bounds: int32 [4, 2], replicated, may hold values from 0 to 64, as said below
- out_grad: bfloat16 [8192, 2048], P('seq', 'fsdp'), may hold values from -6 to 6
Outputs:
- mixed: bfloat16 [8192, 2048], P('seq', 'fsdp')
- query_grad: bfloat16 [8192, 2048], P('seq', 'fsdp')
- key_grad: bfloat16 [8192, 2048], P('seq', 'fsdp')
- value_grad: bfloat16 [8192, 2048], P('seq', 'fsdp')
- weight_grad: float32 [16, 128, 128], P(None, 'fsdp', 'seq')
- gain_grad: float32 [16, 128], P('fsdp')
Inputs may be any that keep to these rules, and one draw needn't show every extreme that they name: `doc_bounds`: the rows list the 4 documents in order: column 0 is the first block and column 1 the block after the last; the first document starts at block 0, each ends where the next starts, the last ends at block 64; every document holds one block or more of 128 tokens.
All inputs are finite; a program needn't handle non-finite values.
Results may differ from a plain program's by a relative error of at most 0.015.
Values may be sent and summed in bfloat16 or wider, within the bound.
A program may use at most 64 MiB of HBM per device.

v0:
```python
import jax
import jax.numpy as jnp
from jax import lax
from jax.sharding import PartitionSpec as P

HS = 128
BLK = 128


epsilon = 1.0


def carried_in(shard, axis, join, neutral, backward):
    count = lax.axis_size(axis)
    place = lax.axis_index(axis)
    ahead = count - 1 - place if backward else place
    gathered = jax.tree.map(
        lambda a, kind: lax.all_gather(a.astype(kind), axis), shard, (jnp.bfloat16, jnp.bfloat16)
    )
    state = jax.tree.map(lambda a, e: jnp.zeros_like(a) + jnp.asarray(e, a.dtype), shard, neutral)

    def one(hop, state):
        source = count - 1 - hop if backward else hop
        return join(
            state,
            jax.tree.map(
                lambda a, own: lax.dynamic_index_in_dim(a, source, 0, False).astype(own.dtype),
                gathered,
                shard,
            ),
        )

    return lax.fori_loop(0, ahead, one, state)


def chain_states(earlier, later):
    early_state, early_flag = earlier
    late_state, late_flag = later
    return (
        jnp.where(late_flag > 0.0, late_state, early_state + late_state),
        jnp.maximum(early_flag, late_flag),
    )


def project(rows, weight):
    return jnp.einsum("bthd,hde->bthe", rows, weight, preferred_element_type=jnp.float32).astype(
        jnp.bfloat16
    )


def local(queries, keys, values, feature_weight, norm_gain, doc_bounds, out_grad):
    rows_full = lax.all_gather(feature_weight, "seq", axis=2, tiled=True)
    weight_local = lax.all_to_all(rows_full, "fsdp", split_axis=0, concat_axis=1, tiled=True)
    head_count = weight_local.shape[0]
    tokens_here = queries.shape[0]
    block_count = tokens_here // BLK
    block_shape = (block_count, BLK, head_count, HS)
    query_blocks = queries.reshape(block_shape)
    key_blocks = keys.reshape(block_shape)
    value_blocks = values.reshape(block_shape)
    qfeat = project(query_blocks, weight_local)
    kfeat = project(key_blocks, weight_local)
    first_block = lax.axis_index("seq") * block_count
    block_ids = first_block + jnp.arange(block_count, dtype=jnp.int32)
    starts = doc_bounds[:, 0]
    starts_here = jnp.any(starts[None, :] == block_ids[:, None], axis=1)
    opened = jnp.cumsum(starts_here.astype(jnp.int32))
    reach_left = opened == 0
    reach_right = opened[-1] - opened == 0
    has_start = jnp.any(starts_here).astype(jnp.float32)
    updates = jnp.einsum("bthe,bthf->bhef", kfeat, value_blocks, preferred_element_type=jnp.float32)
    zero_state = jnp.zeros(updates.shape[1:], jnp.float32)
    zero_flag = jnp.zeros((), jnp.float32)
    running = zero_state
    prefix_list = []
    for position in range(block_count):
        held = jnp.where(starts_here[position], zero_state, running)
        prefix_list.append(held)
        running = held + updates[position]
    entering, _ = carried_in(
        (running, has_start), "seq", chain_states, (zero_state, zero_flag), False
    )
    states = jnp.stack(prefix_list) + jnp.where(
        reach_left[:, None, None, None], entering[None], 0.0
    )
    state_half = states.astype(jnp.bfloat16)
    causal = jnp.arange(BLK)[:, None] >= jnp.arange(BLK)[None, :]
    scores = jnp.einsum("bthe,bshe->bhts", qfeat, kfeat, preferred_element_type=jnp.float32)
    prob_half = jnp.where(causal, scores, 0.0).astype(jnp.bfloat16)
    mixed_f = jnp.einsum("bthe,bhef->bthf", qfeat, state_half, preferred_element_type=jnp.float32)
    mixed_f = mixed_f + jnp.einsum(
        "bhts,bshf->bthf", prob_half, value_blocks, preferred_element_type=jnp.float32
    )
    gains = norm_gain.astype(jnp.float32)
    inverse = lax.rsqrt(jnp.mean(mixed_f * mixed_f, axis=-1, keepdims=True) + epsilon)
    mixed = (mixed_f * inverse * gains).astype(jnp.bfloat16)
    grad_y = out_grad.reshape(block_shape).astype(jnp.float32)
    scaled = grad_y * gains
    grad_mix = inverse * (
        scaled - mixed_f * inverse * inverse * jnp.mean(scaled * mixed_f, axis=-1, keepdims=True)
    )
    grad_half = grad_mix.astype(jnp.bfloat16)
    gain_part = jnp.sum(grad_y * mixed_f * inverse, axis=(0, 1))
    state_grads = jnp.einsum(
        "bthe,bthf->bhef", qfeat, grad_half, preferred_element_type=jnp.float32
    )
    running = zero_state
    suffix_list = [zero_state] * block_count
    for position in reversed(range(block_count)):
        suffix_list[position] = running
        running = jnp.where(starts_here[position], zero_state, running + state_grads[position])
    leaving, _ = carried_in(
        (running, has_start), "seq", chain_states, (zero_state, zero_flag), True
    )
    suffix = jnp.stack(suffix_list) + jnp.where(
        reach_right[:, None, None, None], leaving[None], 0.0
    )
    suffix_half = suffix.astype(jnp.bfloat16)
    dot_grads = jnp.einsum(
        "bthf,bshf->bhts", grad_half, value_blocks, preferred_element_type=jnp.float32
    )
    dot_half = jnp.where(causal, dot_grads, 0.0).astype(jnp.bfloat16)
    qfeat_grad = jnp.einsum(
        "bthf,bhef->bthe", grad_half, state_half, preferred_element_type=jnp.float32
    )
    qfeat_grad = (
        qfeat_grad
        + jnp.einsum("bhts,bshe->bthe", dot_half, kfeat, preferred_element_type=jnp.float32)
    ).astype(jnp.bfloat16)
    kfeat_grad = jnp.einsum(
        "bshf,bhef->bshe", value_blocks, suffix_half, preferred_element_type=jnp.float32
    )
    kfeat_grad = (
        kfeat_grad
        + jnp.einsum("bhts,bthe->bshe", dot_half, qfeat, preferred_element_type=jnp.float32)
    ).astype(jnp.bfloat16)
    value_grad = jnp.einsum(
        "bshe,bhef->bshf", kfeat, suffix_half, preferred_element_type=jnp.float32
    )
    value_grad = (
        value_grad
        + jnp.einsum("bhts,bthf->bshf", prob_half, grad_half, preferred_element_type=jnp.float32)
    ).astype(jnp.bfloat16)
    query_grad = jnp.einsum(
        "bthe,hde->bthd", qfeat_grad, weight_local, preferred_element_type=jnp.float32
    ).astype(jnp.bfloat16)
    key_grad = jnp.einsum(
        "bthe,hde->bthd", kfeat_grad, weight_local, preferred_element_type=jnp.float32
    ).astype(jnp.bfloat16)
    weight_part = jnp.einsum(
        "bthd,bthe->hde", query_blocks, qfeat_grad, preferred_element_type=jnp.float32
    )
    weight_part = weight_part + jnp.einsum(
        "bthd,bthe->hde", key_blocks, kfeat_grad, preferred_element_type=jnp.float32
    )
    weight_sum, gain_sum = lax.psum((weight_part, gain_part), "seq")
    column_width = weight_sum.shape[2] // lax.axis_size("seq")
    weight_columns = lax.dynamic_slice_in_dim(
        weight_sum, lax.axis_index("seq") * column_width, column_width, 2
    )
    owned_grad = lax.all_to_all(weight_columns, "fsdp", split_axis=1, concat_axis=0, tiled=True)
    factor = (lax.axis_size("seq") * tokens_here) ** (-0.5)
    flat_shape = (tokens_here, head_count * HS)
    return (
        mixed.reshape(flat_shape),
        query_grad.reshape(flat_shape),
        key_grad.reshape(flat_shape),
        value_grad.reshape(flat_shape),
        owned_grad * factor,
        gain_sum * factor,
    )


def solution(mesh):
    placed = (
        P("seq", "fsdp"),
        P("seq", "fsdp"),
        P("seq", "fsdp"),
        P(None, "fsdp", "seq"),
        P("fsdp", None),
        P(),
        P("seq", "fsdp"),
    )
    return jax.shard_map(
        local,
        mesh=mesh,
        in_specs=placed,
        out_specs=(
            P("seq", "fsdp"),
            P("seq", "fsdp"),
            P("seq", "fsdp"),
            P("seq", "fsdp"),
            P(None, "fsdp", "seq"),
            P("fsdp", None),
        ),
        check_vma=False,
    )
```

profile of v0, /device:TPU:0, one launch (start us, length us, event | category | flops | bytes accessed | tf_op | source)
XLA Modules:
  0.0 343.1 jit_solution(11068961208618551254)
XLA Ops:
  8.1 24.6 %all_gather.19 = bf16[16,64,128]{1,0,2:T(8,128)(2,1)S(1)} all-gather(bf16[16,64,8]{1,0,2:T(8,128)(2,1)S(1)} %copy.146), channel_id=1, replica_groups=mesh['seq'=16,'fsdp'=2] {'seq'}, dimensions={2}, use_global_device_ids=true | all-gather | bytes 278528 | tf_op jit(solution)/shard_map/all_gather | solution.py:52
  32.7 1.1 copy.147
  33.8 3.4 %all-to-all-start = ((bf16[16,64,128]{2,1,0:T(8,128)(2,1)}), bf16[16,64,128]{2,1,0:T(8,128)(2,1)S(1)}, u32[]{:S(2)}, u32[]{:S(2)}) async-start(bf16[16,64,128]{2,1,0:T(8,128)(2,1)} %copy.147), calls=%async_computation | async-start | bytes 524288 | tf_op jit(solution)/shard_map/all_to_all | solution.py:53
  40.1 3.1 all-to-all-done
  44.7 1.4 copy-done
  46.1 2.9 fusion.38
  51.1 29.8 %all-reduce = bf16[16]{0:T(256)(128)(2,1)S(1)} all-reduce(bf16[16]{0:T(256)(128)(2,1)S(1)} %dynamic-update-slice), channel_id=1, replica_groups=mesh['seq'=16,'fsdp'=2] {'seq'}, use_global_device_ids=true, to_apply=%add | all-reduce | flops 16 | bytes 64
  81.7 1.2 copy.208
  83.2 1.9 copy.210
  85.1 1.9 copy.161
  87.9 2.6 fusion.39
  91.9 1.6 select_convert_fusion.1
  93.5 2.5 all-gather.3.cloned.1.call-done
  96.1 2.4 fusion.21
  100.3 1.7 multiply_convert_fusion
  103.0 3.6 %fusion.35 = (bf16[1,8,128,128]{3,2,1,0:T(8,128)(2,1)}, f32[1,8,128,128]{3,2,1,0:T(8,128)}, f32[1,8,128,128]{3,2,1,0:T(8,128)}) fusion(f32[4,8,128,128]{3,2,1,0:T(8,128)S(1)} %fusion.18, pred[]{:T(512)} %bitcast.29, pred[]{:T(512)} %bitcast.7, pred[]{:T(512)} %bitcast.13, pred[]{:T(512)} %bitcast.14), kind=kLoop, calls=%fused_computation.62 | loop fusion | flops 1048576 | bytes 3407876 | tf_op jit(solution)/shard_map/convert_element_type | solution.py:18
  106.9 2.6 select_convert_fusion
  112.5 1.7 copy.167
  114.2 2.4 copy.160
  116.6 67.7 %psum.15 = f32[8,128]{1,0:T(8,128)S(1)} all-reduce(f32[8,128]{1,0:T(8,128)S(1)} %get-tuple-element.136), channel_id=1, replica_groups=mesh['seq'=16,'fsdp'=2] {'seq'}, use_global_device_ids=true, to_apply=%region_11.12 | all-reduce | flops 1024 | bytes 8192 | tf_op jit(solution)/shard_map/psum | solution.py:156
  184.9 1.5 fusion.36
  186.3 3.1 copy_bitcast_fusion.2
  189.4 1.8 all-gather.5.cloned.1.call-done
  191.3 37.6 %while.27 = (s32[]{:T(128)}, f32[8,128,128]{2,1,0:T(8,128)S(1)}, s32[]{:T(128)}, bf16[16]{0:T(256)(128)(2,1)S(1)}, bf16[16,8,128,128]{3,2,1,0:T(8,128)(2,1)}, /*...) while((s32[]{:T(128)}, f32[8,128,128]{2,1,0:T(8,128)S(1)}, s32[]{:T(128)}, ...), condition=%wide.region_8.9_spmd, body=%wide.region_7.8_spmd.sunk | while | flops 393223 | bytes 1310887 | solution.py:33
  192.7 1.1 add_select_fusion.5
  195.2 1.1 add_select_fusion.5
  197.7 1.1 add_select_fusion.5
  200.2 1.1 add_select_fusion.5
  202.7 1.1 add_select_fusion.5
  205.2 1.1 add_select_fusion.5
  207.7 1.1 add_select_fusion.5
  210.2 1.1 add_select_fusion.5
  212.7 1.1 add_select_fusion.5
  215.3 1.1 add_select_fusion.5
  217.8 1.1 add_select_fusion.5
  220.3 1.1 add_select_fusion.5
  222.8 1.1 add_select_fusion.5
  225.3 1.1 add_select_fusion.5
  227.8 1.1 add_select_fusion.5
  229.0 2.4 fusion.24
  234.3 2.0 fusion.29
  236.3 1.3 fusion.10
  237.6 1.7 copy.173
  239.3 2.1 fusion.8
  242.1 82.9 %all-reduce.3.cloned.1.call-done = f32[8,128,128]{1,2,0:T(8,128)} async-done(((f32[8,128,128]{1,2,0:T(8,128)}), f32[8,128,128]{1,2,0:T(8,128)}) %all-reduce.3.cloned.1.call-update) | async-done | bytes 524304 | tf_op jit(solution)/shard_map/psum | solution.py:156
  326.9 3.3 all-to-all-start.1
  330.2 1.8 copy_bitcast_fusion
  332.0 2.1 all-to-all-done.1
  (146 shorter events, 34.5 us)
Async XLA Ops:
  7.2 31.5 %copy-start.28 = (bf16[512,1024]{1,0:T(8,128)(2,1)S(1)}, bf16[512,1024]{1,0:T(8,128)(2,1)}, u32[]{:S(2)}) copy-start(bf16[512,1024]{1,0:T(8,128)(2,1)} %param.12) | copy-start | bytes 3145732
  7.2 31.8 %copy-start.29 = (bf16[512,1024]{1,0:T(8,128)(2,1)S(1)}, bf16[512,1024]{1,0:T(8,128)(2,1)}, u32[]{:S(2)}) copy-start(bf16[512,1024]{1,0:T(8,128)(2,1)} %param.13) | copy-start | bytes 3145732
  33.8 9.4 %all-to-all-start = ((bf16[16,64,128]{2,1,0:T(8,128)(2,1)}), bf16[16,64,128]{2,1,0:T(8,128)(2,1)S(1)}, u32[]{:S(2)}, u32[]{:S(2)}) async-start(bf16[16,64,128]{2,1,0:T(8,128)(2,1)} %copy.147), calls=%async_computation | async-start | bytes 524288 | tf_op jit(solution)/shard_map/all_to_all | solution.py:53
  37.3 58.7 %all-gather.3.cloned.1.call-start = ((), (), s32[]{:S(2)}) async-start(), calls=%async_computation.2 | async-start | bytes 4456448 | tf_op jit(solution)/shard_map/all_gather | solution.py:18
  39.0 4.7 %copy-start.5 = (bf16[64,8,8,128]{3,2,1,0:T(8,128)(2,1)}, bf16[64,8,8,128]{3,2,1,0:T(8,128)(2,1)S(1)}, u32[]{:S(2)}) copy-start(bf16[64,8,8,128]{3,2,1,0:T(8,128)(2,1)S(1)} %copy.206) | copy-start | bytes 3145732
  39.3 4.9 %copy-start.17 = (bf16[64,8,8,128]{3,2,1,0:T(8,128)(2,1)}, bf16[64,8,8,128]{3,2,1,0:T(8,128)(2,1)S(1)}, u32[]{:S(2)}) copy-start(bf16[64,8,8,128]{3,2,1,0:T(8,128)(2,1)S(1)} %copy.207) | copy-start | bytes 3145732
  43.7 1.0 copy-start.7
  44.7 1.4 copy-start
  44.7 5.0 %copy-start.39 = (u32[32]{0:T(128)S(1)}, u32[32]{0:T(128)}, u32[]{:S(2)}) copy-start(u32[32]{0:T(128)} %constant.96) | copy-start | bytes 388
  44.7 37.0 %copy-start.30 = (bf16[512,1024]{1,0:T(8,128)(2,1)S(1)}, bf16[512,1024]{1,0:T(8,128)(2,1)}, u32[]{:S(2)}) copy-start(bf16[512,1024]{1,0:T(8,128)(2,1)} %param.11) | copy-start | bytes 3145732
  46.1 36.9 %copy-start.27 = (bf16[512,1024]{1,0:T(8,128)(2,1)S(1)}, bf16[512,1024]{1,0:T(8,128)(2,1)}, u32[]{:S(2)}) copy-start(bf16[512,1024]{1,0:T(8,128)(2,1)} %param.17) | copy-start | bytes 3145732
  49.0 142.2 %all-gather.5.cloned.1.call-start = ((), (), s32[]{:S(2)}) async-start(), calls=%async_computation.3 | async-start | bytes 4456448 | tf_op jit(solution)/shard_map/all_gather | solution.py:18
  85.1 1.9 copy-start.38
  87.0 3.4 copy-start.3
  87.1 4.9 %copy-start.8 = (bf16[4,128,8,128]{1,3,0,2:T(8,128)(2,1)S(1)}, bf16[4,128,8,128]{1,3,0,2:T(8,128)(2,1)}, u32[]{:S(2)}) copy-start(bf16[4,128,8,128]{1,3,0,2:T(8,128)(2,1)} %copy-done.7) | copy-start | bytes 3145732
  91.0 1.0 copy-start.11
  96.1 2.5 copy-start.31
  96.1 2.5 copy-start.18
  96.1 2.5 copy-start.22
  100.3 1.7 copy-start.12
  102.0 1.0 copy-start.14
  106.7 218.4 %all-reduce.3.cloned.1.call-start = ((), (), s32[]{:S(2)}) async-start(), calls=%async_computation.4 | async-start | bytes 1048576 | tf_op jit(solution)/shard_map/psum | solution.py:156
  106.9 2.6 copy-start.15
  106.9 2.6 copy-start.32
  106.9 2.6 copy-start.34
  106.9 2.6 copy-start.36
  109.5 1.0 copy-start.20
  109.5 1.6 copy-start.9
  112.0 2.2 copy-start.1
  112.5 72.4 %copy-start.26 = (f32[1,8,128,128]{3,2,1,0:T(8,128)S(1)}, f32[1,8,128,128]{3,2,1,0:T(8,128)}, u32[]{:S(2)}) copy-start(f32[1,8,128,128]{3,2,1,0:T(8,128)} %get-tuple-element.161) | copy-start | bytes 1572868
  184.3 2.1 copy-start.25
  191.3 37.7 %copy-start.19 = (bf16[64,8,8,128]{3,2,1,0:T(8,128)(2,1)S(1)}, bf16[64,8,8,128]{3,2,1,0:T(8,128)(2,1)}, u32[]{:S(2)}) copy-start(bf16[64,8,8,128]{3,2,1,0:T(8,128)(2,1)} %copy-done.17) | copy-start | bytes 3145732
  228.9 2.4 copy-start.13
  229.0 2.4 copy-start.21
  231.4 1.2 copy-start.6
  232.6 1.2 copy-start.10
  232.6 1.4 copy-start.33
  232.6 1.5 copy-start.35
  232.6 1.7 copy-start.37
  234.3 2.0 copy-start.2
  234.3 2.0 copy-start.4
  237.6 1.7 copy-start.16
  237.6 1.7 copy-start.23
  241.4 88.8 %copy-start.24 = (bf16[4,128,8,128]{3,2,1,0:T(8,128)(2,1)S(1)}, bf16[4,128,8,128]{3,2,1,0:T(8,128)(2,1)}, u32[]{:S(2)}) copy-start(bf16[4,128,8,128]{3,2,1,0:T(8,128)(2,1)} %copy.173) | copy-start | bytes 3145732
  326.9 7.2 %all-to-all-start.1 = ((f32[2,1,4096]{2,1,0:T(1,128)}), f32[2,1,4096]{2,1,0:T(1,128)S(1)}, u32[]{:S(2)}, u32[]{:S(2)}) async-start(f32[2,1,4096]{2,1,0:T(1,128)} %reshape.121), calls=%async_computation.1 | async-start | bytes 65536 | tf_op jit(solution)/shard_map/all_to_all | solution.py:161
Sparse Core Ops, SparseCore 0:
  49.2 46.7 all-gather.2
  106.8 84.4 all-gather.4
  237.7 87.2 all-reduce.2
where the time goes:
time: 345 us; the launch traced here: 343 us
  blocking collectives  122 us (35%)
  waiting for transfers between devices  92.4 us (27%)
  local copies, waits for them, and re-layouts  41.6 us (12%)
  other arithmetic  33.2 us (10%)
  matrix products  20.9 us (6%)
  between operations  15 us (4%)
  loops' own time  10.9 us (3%)
  starting transfers between devices  7.01 us (2%)
    psum x1, waiting for transfers between devices, local(): weight_sum, gain_sum = lax.psum((weight_part, gain_part), 'seq')  82.9 us
    psum x1, blocking collectives, local(): weight_sum, gain_sum = lax.psum((weight_part, gain_part), 'seq')  67.7 us
    unnamed x1, blocking collectives  29.8 us
    all_gather x1, blocking collectives, local(): rows_full = lax.all_gather(feature_weight, 'seq', axis=2, tiled=True)  24.6 us
    select_n x15, other arithmetic, chain_states(): jnp.where(late_flag > 0.0, late_state, early_state + late_state)  16.8 us
    unnamed x90, local copies, waits for them, and re-layouts  12.7 us
    another operation x2, loops' own time, carried_in(): return lax.fori_loop(0, ahead, one, state)  10.9 us
    dynamic_slice x15, local copies, waits for them, and re-layouts, one(): lax.dynamic_index_in_dim(a, source, 0, False).astype(own.dtype)  9.95 us
  transfers between devices with their start and end apart: 5, of which 5 were waited for; matrix products, arithmetic and copies ran while one was open for 10% of the time, Pallas kernels for 0%

commit v1 on v0

--- a/solution.py
+++ b/solution.py
@@ -1,6 +1,10 @@
+import functools
+
 import jax
 import jax.numpy as jnp
 from jax import lax
+from jax.experimental import pallas as pl
+from jax.experimental.pallas import tpu as pltpu
 from jax.sharding import PartitionSpec as P
 
 HS = 128
@@ -48,7 +52,7 @@
     )
 
 
-def local(queries, keys, values, feature_weight, norm_gain, doc_bounds, out_grad):
+def plain(queries, keys, values, feature_weight, norm_gain, doc_bounds, out_grad):
     rows_full = lax.all_gather(feature_weight, "seq", axis=2, tiled=True)
     weight_local = lax.all_to_all(rows_full, "fsdp", split_axis=0, concat_axis=1, tiled=True)
     head_count = weight_local.shape[0]
@@ -170,6 +174,406 @@
         gain_sum * factor,
     )
 
+MESH = pl.DeviceIdType.MESH
+
+
+def nn(a, b):
+    return lax.dot_general(a, b, (((1,), (0,)), ((), ())), preferred_element_type=jnp.float32)
+
+
+def nt(a, b):
+    return lax.dot_general(a, b, (((1,), (1,)), ((), ())), preferred_element_type=jnp.float32)
+
+
+def tn(a, b):
+    return lax.dot_general(a, b, (((0,), (0,)), ((), ())), preferred_element_type=jnp.float32)
+
+
+def layer_kernel(
+    n, heads, blocks, docs, factor,
+    bounds, q, k, v, og, gain, wx,
+    mixed, qgrad, kgrad, vgrad, wout, gout,
+    gain_f, wslab, wpart, gw, wt, mloc, mtot, rx, tx, back,
+    qf, kf, prob, oin, sh, dh, eloc, etot, rx2, tx2, back2,
+    dotq, dqf, dkf, dkp, vgp, wgt, wgs, rwg, gl, gp, fin, rfin,
+    w_s, w_r, g_s, g_r, m_s, m_r, b_s, b_r, e_s, e_r, c_s, c_r, p_s, p_r, t_s, t_r, f_s, f_r,
+):
+    me = lax.axis_index("seq")
+    mine = lax.axis_index("fsdp")
+    partner = 1 - mine
+    per_head = n // heads
+    slab = HS // per_head
+    width = HS // n
+    groups = t_s.shape[0]
+    group_rows = heads * width // groups
+
+    barrier = pltpu.get_barrier_semaphore()
+
+    def greet(step, carry):
+        pl.semaphore_signal(
+            barrier, inc=1, device_id={"seq": lax.rem(me + step, n)}, device_id_type=MESH
+        )
+        return carry
+
+    lax.fori_loop(1, n, greet, 0)
+    pl.semaphore_signal(barrier, inc=1, device_id={"fsdp": partner}, device_id_type=MESH)
+
+    def push(src, dst, send, recv, p):
+        return pltpu.make_async_remote_copy(
+            src_ref=src, dst_ref=dst, send_sem=send, recv_sem=recv,
+            device_id={"seq": p}, device_id_type=MESH,
+        )
+
+    def opens_in(first, count):
+        found = jnp.float32(0.0)
+        for i in range(docs):
+            s = bounds[i, 0]
+            found = jnp.where(jnp.logical_and(s >= first, s < first + count), 1.0, found)
+        return found
+
+    def columns(h):
+        return pl.ds(pl.multiple_of(h * HS, HS), HS)
+
+    def rows(b):
+        return pl.ds(b * BLK, BLK)
+
+    cont = [1.0 - opens_in(me * blocks + b, 1) for b in range(blocks)]
+    reach_left = []
+    value = jnp.float32(1.0)
+    for b in range(blocks):
+        value = value * cont[b]
+        reach_left.append(value)
+    reach_right = [None] * blocks
+    value = jnp.float32(1.0)
+    for b in reversed(range(blocks)):
+        reach_right[b] = value
+        value = value * cont[b]
+
+    gain_f[...] = gain[...].astype(jnp.float32)
+
+    def outer_products(h, carry):
+        run = jnp.zeros((HS, HS), jnp.float32)
+        for b in range(blocks):
+            held = run * cont[b]
+            mloc[b, h] = held
+            run = held + tn(k[rows(b), columns(h)], v[rows(b), columns(h)])
+        mtot[pl.ds(h * per_head, per_head)] = run.reshape(per_head, slab, HS).astype(jnp.bfloat16)
+        return carry
+
+    lax.fori_loop(0, heads, outer_products, 0)
+    pl.semaphore_wait(barrier, n)
+
+    weight_swap = pltpu.make_async_remote_copy(
+        src_ref=wx.at[partner], dst_ref=wpart, send_sem=w_s, recv_sem=w_r,
+        device_id={"fsdp": partner}, device_id_type=MESH,
+    )
+    weight_swap.start()
+
+    def send_totals(step, carry):
+        p = lax.rem(me + step, n)
+        push(mtot.at[p], rx.at[me], m_s.at[p], m_r.at[me], p).start()
+        return carry
+
+    lax.fori_loop(1, n, send_totals, 0)
+    weight_swap.wait()
+    lane = lax.broadcasted_iota(jnp.int32, wslab.shape, 1)
+    own_lane = (lane // (HS // 2)) == mine
+    wslab[...] = jnp.where(
+        own_lane, wx[mine].astype(jnp.float32), wpart[...].astype(jnp.float32)
+    ).astype(jnp.bfloat16)
+
+    def send_weights(step, carry):
+        p = lax.rem(me + step, n)
+        push(wslab, gw.at[me], g_s.at[p], g_r.at[me], p).start()
+        return carry
+
+    lax.fori_loop(1, n, send_weights, 0)
+    gw[me] = wslab[...]
+
+    def scan(total, arrived, parts, entered, in_s, in_r, out_s, out_r, backward):
+        arrived[me] = total[me]
+
+        def one(step, state):
+            p = n - 1 - step if backward else step
+
+            @pl.when(p != me)
+            def _():
+                push(total.at[p], arrived.at[p], in_s.at[p], in_r.at[p], p).wait_recv()
+
+            parts[p] = state.astype(jnp.bfloat16)
+
+            @pl.when(p != me)
+            def _():
+                push(parts.at[p], entered.at[me], out_s.at[p], out_r.at[me], p).start()
+
+            keep = 1.0 - opens_in(p * blocks, blocks)
+            return state * keep + arrived[p].astype(jnp.float32)
+
+        lax.fori_loop(0, n, one, jnp.zeros((slab, HS), jnp.float32))
+        entered[me] = parts[me]
+
+    def entering(h, parts, entered, out_s, out_r):
+        for j in range(per_head):
+            p = h * per_head + j
+
+            @pl.when(p != me)
+            def _():
+                push(parts.at[p], entered.at[p], out_s.at[p], out_r.at[p], p).wait_recv()
+
+        return entered[pl.ds(h * per_head, per_head)].astype(jnp.float32).reshape(HS, HS)
+
+    scan(mtot, rx, tx, back, m_s, m_r, b_s, b_r, False)
+
+    def await_weights(step, carry):
+        p = lax.rem(me + n - step, n)
+        push(wslab, gw.at[p], g_s.at[p], g_r.at[p], p).wait_recv()
+        return carry
+
+    lax.fori_loop(1, n, await_weights, 0)
+    causal = lax.broadcasted_iota(jnp.int32, (BLK, BLK), 0) >= lax.broadcasted_iota(
+        jnp.int32, (BLK, BLK), 1
+    )
+
+    def project_pair(pair, carry):
+        both = gw[:, pl.ds(pl.multiple_of(pair * 2 * width, 2 * width), 2 * width), :]
+        both = both.astype(jnp.float32)
+        for j in range(2):
+            h = 2 * pair + j
+            weight = both[:, j * width : (j + 1) * width, :].reshape(HS, HS).astype(jnp.bfloat16)
+            wt[h] = weight
+            qh = nt(q[:, columns(h)], weight).astype(jnp.bfloat16)
+            kh = nt(k[:, columns(h)], weight).astype(jnp.bfloat16)
+            qf[h] = qh
+            kf[h] = kh
+            for b in range(blocks):
+                at = slice(b * BLK, (b + 1) * BLK)
+                scores = jnp.where(causal, nt(qh[at], kh[at]), 0.0).astype(jnp.bfloat16)
+                prob[h, rows(b), :] = scores
+                oin[h, rows(b), :] = nn(scores, v[rows(b), columns(h)])
+        return carry
+
+    lax.fori_loop(0, heads // 2, project_pair, 0)
+
+    def forward(h, carry):
+        enter = entering(h, tx, back, b_s, b_r)
+        weight = wt[h]
+        g = gain_f[pl.ds(h, 1), :]
+        terms = []
+        gain_sum = jnp.zeros((1, HS), jnp.float32)
+        for b in range(blocks):
+            memory = (mloc[b, h] + reach_left[b] * enter).astype(jnp.bfloat16)
+            state = nn(weight, memory).astype(jnp.bfloat16)
+            sh[b, h] = state
+            qb = qf[h, rows(b), :]
+            o = oin[h, rows(b), :] + nn(qb, state)
+            r = lax.rsqrt(jnp.mean(o * o, axis=-1, keepdims=True) + epsilon)
+            normed = o * r
+            mixed[rows(b), columns(h)] = (normed * g).astype(jnp.bfloat16)
+            gy = og[rows(b), columns(h)].astype(jnp.float32)
+            scaled = gy * g
+            inner = jnp.mean(scaled * o, axis=-1, keepdims=True)
+            d = (r * (scaled - normed * (r * inner))).astype(jnp.bfloat16)
+            dh[h, rows(b), :] = d
+            gain_sum = gain_sum + jnp.sum(gy * normed, axis=0, keepdims=True)
+            terms.append(tn(qb, d))
+        gl[pl.ds(h, 1), :] = gain_sum
+        run = jnp.zeros((HS, HS), jnp.float32)
+        for b in reversed(range(blocks)):
+            eloc[b, h] = run
+            run = (run + terms[b]) * cont[b]
+        etot[pl.ds(h * per_head, per_head)] = run.reshape(per_head, slab, HS).astype(jnp.bfloat16)
+        for j in range(per_head):
+            p = h * per_head + j
+
+            @pl.when(p != me)
+            def _():
+                push(etot.at[p], rx2.at[me], e_s.at[p], e_r.at[me], p).start()
+
+        return carry
+
+    lax.fori_loop(0, heads, forward, 0)
+
+    def send_gain(step, carry):
+        p = lax.rem(me + step, n)
+        push(gl, gp.at[me], p_s.at[p], p_r.at[me], p).start()
+        return carry
+
+    lax.fori_loop(1, n, send_gain, 0)
+    gp[me] = gl[...]
+
+    def query_side(h, carry):
+        for b in range(blocks):
+            d = dh[h, rows(b), :]
+            scores = jnp.where(causal, nt(d, v[rows(b), columns(h)]), 0.0).astype(jnp.bfloat16)
+            dotq[h, rows(b), :] = scores
+            dqf[rows(b), :] = (nt(d, sh[b, h]) + nn(scores, kf[h, rows(b), :])).astype(jnp.bfloat16)
+        grads = dqf[...]
+        qgrad[:, columns(h)] = nn(grads, wt[h]).astype(jnp.bfloat16)
+        wgt[h] = tn(grads, q[:, columns(h)])
+        return carry
+
+    lax.fori_loop(0, heads, query_side, 0)
+    scan(etot, rx2, tx2, back2, e_s, e_r, c_s, c_r, True)
+
+    def local_key_side(h, carry):
+        for b in range(blocks):
+            dkp[h, rows(b), :] = tn(dotq[h, rows(b), :], qf[h, rows(b), :])
+            vgp[h, rows(b), :] = tn(prob[h, rows(b), :], dh[h, rows(b), :])
+        return carry
+
+    lax.fori_loop(0, heads, local_key_side, 0)
+
+    def key_side(h):
+        enter = entering(h, tx2, back2, c_s, c_r)
+        for b in range(blocks):
+            memory = (eloc[b, h] + reach_right[b] * enter).astype(jnp.bfloat16)
+            vb = v[rows(b), columns(h)]
+            dkf[rows(b), :] = (nt(vb, memory) + dkp[h, rows(b), :]).astype(jnp.bfloat16)
+            vgrad[rows(b), columns(h)] = (
+                nn(kf[h, rows(b), :], memory) + vgp[h, rows(b), :]
+            ).astype(jnp.bfloat16)
+        grads = dkf[...]
+        kgrad[:, columns(h)] = nn(grads, wt[h]).astype(jnp.bfloat16)
+        return (wgt[h] + tn(grads, k[:, columns(h)])).reshape(n, width, HS)
+
+    pairs = heads // 2 // groups
+
+    def key_group(group, carry):
+        def key_pair(i, inner):
+            pair = group * pairs + i
+            both = jnp.concatenate([key_side(2 * pair), key_side(2 * pair + 1)], axis=1)
+            wgs[group, :, pl.ds(pl.multiple_of(i * 2 * width, 2 * width), 2 * width), :] = (
+                both.astype(jnp.bfloat16)
+            )
+            return inner
+
+        lax.fori_loop(0, pairs, key_pair, 0)
+
+        def send_terms(step, inner):
+            p = lax.rem(me + step, n)
+            push(
+                wgs.at[group, p], rwg.at[group, me], t_s.at[group, p], t_r.at[group, me], p
+            ).start()
+            return inner
+
+        lax.fori_loop(1, n, send_terms, 0)
+        rwg[group, me] = wgs[group, me]
+        return carry
+
+    lax.fori_loop(0, groups, key_group, 0)
+
+    def add_gain(step, carry):
+        p = lax.rem(me + n - step, n)
+        push(gl, gp.at[p], p_s.at[p], p_r.at[p], p).wait_recv()
+        return carry
+
+    lax.fori_loop(1, n, add_gain, 0)
+    gout[...] = jnp.sum(gp[...], axis=0) * factor
+
+    for group in range(groups):
+
+        def arrive(step, total):
+            p = lax.rem(me + n - step, n)
+            push(
+                wgs.at[group, p], rwg.at[group, p], t_s.at[group, p], t_r.at[group, p], p
+            ).wait_recv()
+            return total + rwg[group, p].astype(jnp.float32)
+
+        total = lax.fori_loop(1, n, arrive, rwg[group, me].astype(jnp.float32))
+        fin[pl.ds(group * group_rows, group_rows), :] = total * factor
+
+    owned_swap = pltpu.make_async_remote_copy(
+        src_ref=fin, dst_ref=rfin, send_sem=f_s, recv_sem=f_r,
+        device_id={"fsdp": partner}, device_id_type=MESH,
+    )
+    owned_swap.start()
+    wout[mine] = fin[...]
+
+    def sent(step, carry):
+        p = lax.rem(me + step, n)
+        push(mtot.at[p], rx.at[me], m_s.at[p], m_r.at[me], p).wait_send()
+        push(wslab, gw.at[me], g_s.at[p], g_r.at[me], p).wait_send()
+        push(tx.at[p], back.at[me], b_s.at[p], b_r.at[me], p).wait_send()
+        push(etot.at[p], rx2.at[me], e_s.at[p], e_r.at[me], p).wait_send()
+        push(tx2.at[p], back2.at[me], c_s.at[p], c_r.at[me], p).wait_send()
+        push(gl, gp.at[me], p_s.at[p], p_r.at[me], p).wait_send()
+        for group in range(groups):
+            push(
+                wgs.at[group, p], rwg.at[group, me], t_s.at[group, p], t_r.at[group, me], p
+            ).wait_send()
+        return carry
+
+    lax.fori_loop(1, n, sent, 0)
+    owned_swap.wait()
+    wout[partner] = rfin[...]
+
+
+def fused(n, queries, keys, values, feature_weight, norm_gain, doc_bounds, out_grad):
+    tokens, features = queries.shape
+    heads = features // HS
+    blocks = tokens // BLK
+    width = HS // n
+    deep = feature_weight.shape[1]
+    rows_each = heads * HS // n
+    slab_rows = heads * width
+    groups = 2
+    turned = jnp.swapaxes(feature_weight, 1, 2).reshape(2, slab_rows, deep)
+    wx = jnp.concatenate([turned, turned], axis=2)
+    factor = float((n * tokens) ** -0.5)
+    bf, f32 = jnp.bfloat16, jnp.float32
+    vm = pltpu.VMEM
+    per = (heads, tokens, HS)
+    slabs = (n, rows_each, HS)
+    scratch = [
+        vm((heads, HS), f32), vm((slab_rows, HS), bf), vm((slab_rows, HS), bf),
+        vm((n, slab_rows, HS), bf), vm((heads, HS, HS), bf),
+        vm((blocks, heads, HS, HS), f32),
+        vm(slabs, bf), vm(slabs, bf), vm(slabs, bf), vm(slabs, bf),
+        vm(per, bf), vm(per, bf), vm(per, bf), vm(per, f32),
+        vm((blocks, heads, HS, HS), bf), vm(per, bf), vm((blocks, heads, HS, HS), f32),
+        vm(slabs, bf), vm(slabs, bf), vm(slabs, bf), vm(slabs, bf),
+        vm(per, bf), vm((tokens, HS), bf), vm((tokens, HS), bf), vm(per, f32), vm(per, f32),
+        vm((heads, HS, HS), f32),
+        vm((groups, n, slab_rows // groups, HS), bf), vm((groups, n, slab_rows // groups, HS), bf),
+        vm((heads, HS), f32), vm((n, heads, HS), f32),
+        vm((slab_rows, HS), f32), vm((slab_rows, HS), f32),
+    ]
+    dma = pltpu.SemaphoreType.DMA
+    sems = [dma, dma] + [dma((n,))] * 12 + [dma((groups, n))] * 2 + [dma, dma]
+    flat = jax.ShapeDtypeStruct((tokens, features), bf)
+    in_vmem = pl.BlockSpec(memory_space=vm)
+    mixed, qgrad, kgrad, vgrad, wout, gout = pl.pallas_call(
+        functools.partial(layer_kernel, n, heads, blocks, doc_bounds.shape[0], factor),
+        out_shape=(
+            flat, flat, flat, flat,
+            jax.ShapeDtypeStruct((2, slab_rows, HS), f32),
+            jax.ShapeDtypeStruct((heads, HS), f32),
+        ),
+        in_specs=[pl.BlockSpec(memory_space=pltpu.SMEM)] + [in_vmem] * 6,
+        out_specs=(in_vmem,) * 6,
+        scratch_shapes=scratch + sems,
+        compiler_params=pltpu.CompilerParams(
+            collective_id=0, has_side_effects=True, vmem_limit_bytes=52 * 2**20
+        ),
+        cost_estimate=pl.CostEstimate(
+            flops=36 * tokens * features * HS, bytes_accessed=16 * tokens * features,
+            transcendentals=0,
+        ),
+        name="layer",
+    )(doc_bounds, queries, keys, values, out_grad, norm_gain, wx)
+    owned = wout.reshape(2 * heads, width, HS)
+    owned = lax.dynamic_slice_in_dim(owned, lax.axis_index("fsdp") * deep, deep, 2)
+    return mixed, qgrad, kgrad, vgrad, jnp.swapaxes(owned, 1, 2), gout
+
+
+def local(*args):
+    n = lax.axis_size("seq")
+    heads = args[0].shape[1] // HS
+    width = HS // n
+    if lax.axis_size("fsdp") == 2 and width == 8 and n % heads == 0 and heads % 4 == 0:
+        return fused(n, *args)
+    return plain(*args)
+
 
 def solution(mesh):
     placed = (

time: 345 us -> 78.8 us (0.23)
  blocking collectives: 122 us -> 0 us
  waiting for transfers between devices: 92.4 us -> 0 us
  Pallas kernels: 0 us -> 69.1 us
  local copies, waits for them, and re-layouts: 41.6 us -> 7.77 us
  other arithmetic: 33.2 us -> 0.92 us
  matrix products: 20.9 us -> 0 us
  between operations: 15 us -> 0.68 us
  loops' own time: 10.9 us -> 0 us
  starting transfers between devices: 7.01 us -> 0 us
    psum x1 -> x0, waiting for transfers between devices: 82.9 us -> none  [local(): weight_sum, gain_sum = lax.psum((weight_part, gain_part), 'seq')]
    pallas_call x0 -> x1, Pallas kernels: none -> 69.1 us  [fused(): pl.pallas_call(functools.partial(layer_kernel, n, heads, blocks, doc_boun...]
    psum x1 -> x0, blocking collectives: 67.7 us -> none  [local(): weight_sum, gain_sum = lax.psum((weight_part, gain_part), 'seq')]
    unnamed x1 -> x0, blocking collectives: 29.8 us -> none
    all_gather x1 -> x0, blocking collectives: 24.6 us -> none  [local(): rows_full = lax.all_gather(feature_weight, 'seq', axis=2, tiled=True)]
    dot_general x18 -> x0, matrix products: 20.9 us -> none  [the longest x1 2.57 us: local(): jnp.einsum('bthf,bshf->bhts', grad_half, value_blocks, preferred_element_...]
    select_n x17 -> x0, other arithmetic: 20.8 us -> none  [the longest x15 16.8 us: chain_states(): jnp.where(late_flag > 0.0, late_state, early_state + late_state)]
    dynamic_slice x17 -> x0, local copies, waits for them, and re-layouts: 10.9 us -> none  [the longest x15 9.95 us: one(): lax.dynamic_index_in_dim(a, source, 0, False).astype(own.dtype)]
  transfers between devices with their start and end apart: 5 -> 0, of which waited for: 5 -> 0; matrix products, arithmetic and copies ran while one was open for 10% -> 0% of each run, Pallas kernels for 0% -> 0%
where the time goes in v1:
time: 78.8 us; the launch traced here: 78.5 us
  Pallas kernels  69.1 us (88%)
  local copies, waits for them, and re-layouts  7.77 us (10%)
  other arithmetic  0.92 us (1%)
    pallas_call x1, Pallas kernels, fused(): pl.pallas_call(functools.partial(layer_kernel, n, heads, blocks, doc_boun...  69.1 us
    unnamed x16, local copies, waits for them, and re-layouts  7.05 us

profile of v1, /device:TPU:0, one launch (start us, length us, event | category | flops | bytes accessed | tf_op | source)
XLA Modules:
  0.0 78.5 jit_solution(123631887541161189)
XLA Ops:
  0.6 0.0 copy-start.4
  0.6 0.9 %pad_maximum_fusion.wx = bf16[2,64,128]{2,1,0:T(8,128)(2,1)S(1)} fusion(bf16[2,64,64]{2,1,0:T(8,128)(2,1)} %bitcast.7), kind=kLoop, calls=%fused_computation.1 | loop fusion | flops 65536 | bytes 49152 | tf_op jit(solution)/shard_map/concatenate | solution.py:521
  1.6 0.0 copy-done.4
  1.6 0.0 copy-start
  1.6 0.1 copy.13.bounds
  1.7 0.6 copy-done
  2.3 69.1 %layer.1 = (bf16[512,1024]{1,0:T(8,128)(2,1)S(1)}, bf16[512,1024]{1,0:T(8,128)(2,1)}, bf16[512,1024]{1,0:T(8,128)(2,1)}, bf16[512,1024]{1,0:T(8,128)(2,1)}, f32[...) custom-call(s32[4,2]{1,0:T(4,128)S(1)} %copy.13.bounds, bf16[512,1024]{1,0:T(8,128)(2,1)} %q.1, bf16[512,1024]{1,0:T(8,128)(2,1)} %k.1, ...), custom_call_target="tpu_custom_call" | custom-call | flops 2415919104 | bytes 8388608 | tf_op jit(solution)/shard_map/layer/pallas_call | solution.py:545
  71.4 0.7 dynamic-slice_bitcast_fusion
  72.1 0.0 copy-start.3
  72.1 1.0 %copy.19 = bf16[512,1024]{1,0:T(8,128)(2,1)} copy(bf16[512,1024]{1,0:T(8,128)(2,1)S(1)} %get-tuple-element.24) | data formatting | bytes 2097152
  73.1 0.6 copy-done.3
  73.7 0.0 copy-start.2
  73.7 1.0 %copy.20 = bf16[512,1024]{1,0:T(8,128)(2,1)} copy(bf16[512,1024]{1,0:T(8,128)(2,1)S(1)} %copy-done.3) | data formatting | bytes 2097152
  74.7 0.6 copy-done.2
  75.3 0.0 copy-start.1
  75.3 1.0 %copy.21 = bf16[512,1024]{1,0:T(8,128)(2,1)} copy(bf16[512,1024]{1,0:T(8,128)(2,1)S(1)} %copy-done.2) | data formatting | bytes 2097152
  76.3 0.6 copy-done.1
  76.9 1.0 %copy.22 = bf16[512,1024]{1,0:T(8,128)(2,1)} copy(bf16[512,1024]{1,0:T(8,128)(2,1)S(1)} %copy-done.1) | data formatting | bytes 2097152
  77.9 0.6 copy.23
Async XLA Ops:
  0.6 0.9 %copy-start.4 = (s32[4,2]{0,1:T(2,128)S(1)}, s32[4,2]{0,1:T(2,128)}, u32[]{:S(2)}) copy-start(s32[4,2]{0,1:T(2,128)} %param.12) | copy-start | bytes 100
  1.6 0.7 copy-start
  72.1 1.6 %copy-start.3 = (bf16[512,1024]{1,0:T(8,128)(2,1)S(1)}, bf16[512,1024]{1,0:T(8,128)(2,1)}, u32[]{:S(2)}) copy-start(bf16[512,1024]{1,0:T(8,128)(2,1)} %get-tuple-element.25) | copy-start | bytes 3145732
  73.7 1.6 %copy-start.2 = (bf16[512,1024]{1,0:T(8,128)(2,1)S(1)}, bf16[512,1024]{1,0:T(8,128)(2,1)}, u32[]{:S(2)}) copy-start(bf16[512,1024]{1,0:T(8,128)(2,1)} %get-tuple-element.26) | copy-start | bytes 3145732
  75.3 1.6 %copy-start.1 = (bf16[512,1024]{1,0:T(8,128)(2,1)S(1)}, bf16[512,1024]{1,0:T(8,128)(2,1)}, u32[]{:S(2)}) copy-start(bf16[512,1024]{1,0:T(8,128)(2,1)} %get-tuple-element.27) | copy-start | bytes 3145732

commit v2 on v1

--- a/solution.py
+++ b/solution.py
@@ -191,12 +191,13 @@
 
 def layer_kernel(
     n, heads, blocks, docs, factor,
-    bounds, q, k, v, og, gain, wx,
-    mixed, qgrad, kgrad, vgrad, wout, gout,
+    bounds, q_in, k_in, v_in, og_in, gain, wx,
+    mixed_out, qgrad_out, kgrad_out, vgrad_out, wout, gout,
+    q, k, v, og, mixed, qgrad, kgrad, vgrad,
     gain_f, wslab, wpart, gw, wt, mloc, mtot, rx, tx, back,
-    qf, kf, prob, oin, sh, dh, eloc, etot, rx2, tx2, back2,
-    dotq, dqf, dkf, dkp, vgp, wgt, wgs, rwg, gl, gp, fin, rfin,
-    w_s, w_r, g_s, g_r, m_s, m_r, b_s, b_r, e_s, e_r, c_s, c_r, p_s, p_r, t_s, t_r, f_s, f_r,
+    qf, kf, prob, sh, dh, eloc, etot, rx2, tx2, back2,
+    dotq, dqf, dkp, vgp, wgt, wgs, rwg, gl, gp, fin, rfin,
+    w_s, w_r, g_s, g_r, m_s, m_r, b_s, b_r, e_s, e_r, c_s, c_r, p_s, p_r, t_s, t_r, f_s, f_r, io,
 ):
     me = lax.axis_index("seq")
     mine = lax.axis_index("fsdp")
@@ -217,6 +218,19 @@
 
     lax.fori_loop(1, n, greet, 0)
     pl.semaphore_signal(barrier, inc=1, device_id={"fsdp": partner}, device_id_type=MESH)
+
+    loads = [
+        pltpu.make_async_copy(a, b, io.at[i])
+        for i, (a, b) in enumerate([(k_in, k), (v_in, v), (q_in, q), (og_in, og)])
+    ]
+    for load in loads:
+        load.start()
+    stores = [
+        pltpu.make_async_copy(a, b, io.at[4 + i])
+        for i, (a, b) in enumerate(
+            [(mixed, mixed_out), (qgrad, qgrad_out), (kgrad, kgrad_out), (vgrad, vgrad_out)]
+        )
+    ]
 
     def push(src, dst, send, recv, p):
         return pltpu.make_async_remote_copy(
@@ -251,16 +265,26 @@
 
     gain_f[...] = gain[...].astype(jnp.float32)
 
-    def outer_products(h, carry):
-        run = jnp.zeros((HS, HS), jnp.float32)
-        for b in range(blocks):
-            held = run * cont[b]
-            mloc[b, h] = held
-            run = held + tn(k[rows(b), columns(h)], v[rows(b), columns(h)])
-        mtot[pl.ds(h * per_head, per_head)] = run.reshape(per_head, slab, HS).astype(jnp.bfloat16)
-        return carry
-
-    lax.fori_loop(0, heads, outer_products, 0)
+    def outer_products(pair, carry):
+        heads_here = (2 * pair, 2 * pair + 1)
+        terms = [
+            [tn(k[rows(b), columns(h)], v[rows(b), columns(h)]) for b in range(blocks)]
+            for h in heads_here
+        ]
+        for h, term in zip(heads_here, terms):
+            run = jnp.zeros((HS, HS), jnp.float32)
+            for b in range(blocks):
+                held = run * cont[b]
+                mloc[b, h] = held
+                run = held + term[b]
+            mtot[pl.ds(h * per_head, per_head)] = run.reshape(per_head, slab, HS).astype(
+                jnp.bfloat16
+            )
+        return carry
+
+    loads[0].wait()
+    loads[1].wait()
+    lax.fori_loop(0, heads // 2, outer_products, 0)
     pl.semaphore_wait(barrier, n)
 
     weight_swap = pltpu.make_async_remote_copy(
@@ -312,15 +336,16 @@
         lax.fori_loop(0, n, one, jnp.zeros((slab, HS), jnp.float32))
         entered[me] = parts[me]
 
-    def entering(h, parts, entered, out_s, out_r):
-        for j in range(per_head):
-            p = h * per_head + j
+    def entering(pair, parts, entered, out_s, out_r):
+        for j in range(2 * per_head):
+            p = pair * 2 * per_head + j
 
             @pl.when(p != me)
             def _():
                 push(parts.at[p], entered.at[p], out_s.at[p], out_r.at[p], p).wait_recv()
 
-        return entered[pl.ds(h * per_head, per_head)].astype(jnp.float32).reshape(HS, HS)
+        both = entered[pl.ds(pair * 2 * per_head, 2 * per_head)].astype(jnp.float32)
+        return [both[:per_head].reshape(HS, HS), both[per_head:].reshape(HS, HS)]
 
     scan(mtot, rx, tx, back, m_s, m_r, b_s, b_r, False)
 
@@ -337,6 +362,7 @@
     def project_pair(pair, carry):
         both = gw[:, pl.ds(pl.multiple_of(pair * 2 * width, 2 * width), 2 * width), :]
         both = both.astype(jnp.float32)
+        features = []
         for j in range(2):
             h = 2 * pair + j
             weight = both[:, j * width : (j + 1) * width, :].reshape(HS, HS).astype(jnp.bfloat16)
@@ -345,45 +371,68 @@
             kh = nt(k[:, columns(h)], weight).astype(jnp.bfloat16)
             qf[h] = qh
             kf[h] = kh
+            features.append((h, qh, kh))
+        for h, qh, kh in features:
             for b in range(blocks):
                 at = slice(b * BLK, (b + 1) * BLK)
-                scores = jnp.where(causal, nt(qh[at], kh[at]), 0.0).astype(jnp.bfloat16)
-                prob[h, rows(b), :] = scores
-                oin[h, rows(b), :] = nn(scores, v[rows(b), columns(h)])
-        return carry
-
+                prob[h, rows(b), :] = jnp.where(causal, nt(qh[at], kh[at]), 0.0).astype(
+                    jnp.bfloat16
+                )
+        return carry
+
+    loads[2].wait()
     lax.fori_loop(0, heads // 2, project_pair, 0)
-
-    def forward(h, carry):
-        enter = entering(h, tx, back, b_s, b_r)
-        weight = wt[h]
-        g = gain_f[pl.ds(h, 1), :]
+    loads[3].wait()
+
+    def forward(pair, carry):
+        enters = entering(pair, tx, back, b_s, b_r)
+        heads_here = (2 * pair, 2 * pair + 1)
+        states = []
+        for h, enter in zip(heads_here, enters):
+            memory = jnp.concatenate(
+                [
+                    (mloc[b, h] + reach_left[b] * enter).astype(jnp.bfloat16)
+                    for b in range(blocks)
+                ],
+                axis=1,
+            )
+            states.append(nn(wt[h], memory).astype(jnp.bfloat16))
+        outs = []
+        for h, state in zip(heads_here, states):
+            sh[h] = state
+            for b in range(blocks):
+                both = jnp.concatenate([qf[h, rows(b), :], prob[h, rows(b), :]], axis=1)
+                held = jnp.concatenate(
+                    [state[:, b * HS : (b + 1) * HS], v[rows(b), columns(h)]], axis=0
+                )
+                outs.append(nn(both, held))
         terms = []
-        gain_sum = jnp.zeros((1, HS), jnp.float32)
-        for b in range(blocks):
-            memory = (mloc[b, h] + reach_left[b] * enter).astype(jnp.bfloat16)
-            state = nn(weight, memory).astype(jnp.bfloat16)
-            sh[b, h] = state
-            qb = qf[h, rows(b), :]
-            o = oin[h, rows(b), :] + nn(qb, state)
-            r = lax.rsqrt(jnp.mean(o * o, axis=-1, keepdims=True) + epsilon)
-            normed = o * r
-            mixed[rows(b), columns(h)] = (normed * g).astype(jnp.bfloat16)
-            gy = og[rows(b), columns(h)].astype(jnp.float32)
-            scaled = gy * g
-            inner = jnp.mean(scaled * o, axis=-1, keepdims=True)
-            d = (r * (scaled - normed * (r * inner))).astype(jnp.bfloat16)
-            dh[h, rows(b), :] = d
-            gain_sum = gain_sum + jnp.sum(gy * normed, axis=0, keepdims=True)
-            terms.append(tn(qb, d))
-        gl[pl.ds(h, 1), :] = gain_sum
-        run = jnp.zeros((HS, HS), jnp.float32)
-        for b in reversed(range(blocks)):
-            eloc[b, h] = run
-            run = (run + terms[b]) * cont[b]
-        etot[pl.ds(h * per_head, per_head)] = run.reshape(per_head, slab, HS).astype(jnp.bfloat16)
-        for j in range(per_head):
-            p = h * per_head + j
+        for i, h in enumerate(heads_here):
+            g = gain_f[pl.ds(h, 1), :]
+            gain_sum = jnp.zeros((1, HS), jnp.float32)
+            for b in range(blocks):
+                o = outs[i * blocks + b]
+                r = lax.rsqrt(jnp.mean(o * o, axis=-1, keepdims=True) + epsilon)
+                normed = o * r
+                mixed[rows(b), columns(h)] = (normed * g).astype(jnp.bfloat16)
+                gy = og[rows(b), columns(h)].astype(jnp.float32)
+                scaled = gy * g
+                inner = jnp.mean(scaled * o, axis=-1, keepdims=True)
+                d = (r * (scaled - normed * (r * inner))).astype(jnp.bfloat16)
+                dh[h, rows(b), :] = d
+                gain_sum = gain_sum + jnp.sum(gy * normed, axis=0, keepdims=True)
+                terms.append(tn(qf[h, rows(b), :], d))
+            gl[pl.ds(h, 1), :] = gain_sum
+        for i, h in enumerate(heads_here):
+            run = jnp.zeros((HS, HS), jnp.float32)
+            for b in reversed(range(blocks)):
+                eloc[b, h] = run
+                run = (run + terms[i * blocks + b]) * cont[b]
+            etot[pl.ds(h * per_head, per_head)] = run.reshape(per_head, slab, HS).astype(
+                jnp.bfloat16
+            )
+        for j in range(2 * per_head):
+            p = pair * 2 * per_head + j
 
             @pl.when(p != me)
             def _():
@@ -391,7 +440,8 @@
 
         return carry
 
-    lax.fori_loop(0, heads, forward, 0)
+    lax.fori_loop(0, heads // 2, forward, 0)
+    stores[0].start()
 
     def send_gain(step, carry):
         p = lax.rem(me + step, n)
@@ -401,47 +451,62 @@
     lax.fori_loop(1, n, send_gain, 0)
     gp[me] = gl[...]
 
-    def query_side(h, carry):
-        for b in range(blocks):
-            d = dh[h, rows(b), :]
-            scores = jnp.where(causal, nt(d, v[rows(b), columns(h)]), 0.0).astype(jnp.bfloat16)
-            dotq[h, rows(b), :] = scores
-            dqf[rows(b), :] = (nt(d, sh[b, h]) + nn(scores, kf[h, rows(b), :])).astype(jnp.bfloat16)
-        grads = dqf[...]
-        qgrad[:, columns(h)] = nn(grads, wt[h]).astype(jnp.bfloat16)
-        wgt[h] = tn(grads, q[:, columns(h)])
-        return carry
-
-    lax.fori_loop(0, heads, query_side, 0)
+    def query_side(pair, carry):
+        heads_here = (2 * pair, 2 * pair + 1)
+        for h in heads_here:
+            scores = []
+            for b in range(blocks):
+                score = nt(dh[h, rows(b), :], v[rows(b), columns(h)])
+                scores.append(jnp.where(causal, score, 0.0).astype(jnp.bfloat16))
+            for b in range(blocks):
+                dotq[h, rows(b), :] = scores[b]
+                dqf[h, rows(b), :] = (
+                    nt(dh[h, rows(b), :], sh[h, :, rows(b)]) + nn(scores[b], kf[h, rows(b), :])
+                ).astype(jnp.bfloat16)
+        return carry
+
+    lax.fori_loop(0, heads // 2, query_side, 0)
     scan(etot, rx2, tx2, back2, e_s, e_r, c_s, c_r, True)
 
-    def local_key_side(h, carry):
-        for b in range(blocks):
-            dkp[h, rows(b), :] = tn(dotq[h, rows(b), :], qf[h, rows(b), :])
-            vgp[h, rows(b), :] = tn(prob[h, rows(b), :], dh[h, rows(b), :])
-        return carry
-
-    lax.fori_loop(0, heads, local_key_side, 0)
-
-    def key_side(h):
-        enter = entering(h, tx2, back2, c_s, c_r)
-        for b in range(blocks):
-            memory = (eloc[b, h] + reach_right[b] * enter).astype(jnp.bfloat16)
-            vb = v[rows(b), columns(h)]
-            dkf[rows(b), :] = (nt(vb, memory) + dkp[h, rows(b), :]).astype(jnp.bfloat16)
-            vgrad[rows(b), columns(h)] = (
-                nn(kf[h, rows(b), :], memory) + vgp[h, rows(b), :]
-            ).astype(jnp.bfloat16)
-        grads = dkf[...]
-        kgrad[:, columns(h)] = nn(grads, wt[h]).astype(jnp.bfloat16)
-        return (wgt[h] + tn(grads, k[:, columns(h)])).reshape(n, width, HS)
+    def local_terms(pair, carry):
+        for h in (2 * pair, 2 * pair + 1):
+            grads = dqf[h]
+            qgrad[:, columns(h)] = nn(grads, wt[h]).astype(jnp.bfloat16)
+            wgt[h] = tn(grads, q[:, columns(h)])
+            for b in range(blocks):
+                dkp[h, rows(b), :] = tn(dotq[h, rows(b), :], qf[h, rows(b), :])
+                vgp[h, rows(b), :] = tn(prob[h, rows(b), :], dh[h, rows(b), :])
+        return carry
+
+    lax.fori_loop(0, heads // 2, local_terms, 0)
+    stores[1].start()
+
+    def key_pair_grads(pair):
+        enters = entering(pair, tx2, back2, c_s, c_r)
+        heads_here = (2 * pair, 2 * pair + 1)
+        grads = []
+        for h, enter in zip(heads_here, enters):
+            parts = []
+            for b in range(blocks):
+                memory = (eloc[b, h] + reach_right[b] * enter).astype(jnp.bfloat16)
+                vb = v[rows(b), columns(h)]
+                parts.append((nt(vb, memory) + dkp[h, rows(b), :]).astype(jnp.bfloat16))
+                vgrad[rows(b), columns(h)] = (
+                    nn(kf[h, rows(b), :], memory) + vgp[h, rows(b), :]
+                ).astype(jnp.bfloat16)
+            grads.append(jnp.concatenate(parts, axis=0))
+        totals = []
+        for h, grad in zip(heads_here, grads):
+            kgrad[:, columns(h)] = nn(grad, wt[h]).astype(jnp.bfloat16)
+            totals.append((wgt[h] + tn(grad, k[:, columns(h)])).reshape(n, width, HS))
+        return jnp.concatenate(totals, axis=1)
 
     pairs = heads // 2 // groups
 
     def key_group(group, carry):
         def key_pair(i, inner):
             pair = group * pairs + i
-            both = jnp.concatenate([key_side(2 * pair), key_side(2 * pair + 1)], axis=1)
+            both = key_pair_grads(pair)
             wgs[group, :, pl.ds(pl.multiple_of(i * 2 * width, 2 * width), 2 * width), :] = (
                 both.astype(jnp.bfloat16)
             )
@@ -461,6 +526,8 @@
         return carry
 
     lax.fori_loop(0, groups, key_group, 0)
+    stores[2].start()
+    stores[3].start()
 
     def add_gain(step, carry):
         p = lax.rem(me + n - step, n)
@@ -504,8 +571,18 @@
         return carry
 
     lax.fori_loop(1, n, sent, 0)
+    for store in stores:
+        store.wait()
     owned_swap.wait()
     wout[partner] = rfin[...]
+
+
+def hand_on(*refs):
+    copies = [pltpu.make_async_copy(refs[i], refs[4 + i], refs[8].at[i]) for i in range(4)]
+    for copy in copies:
+        copy.start()
+    for copy in copies:
+        copy.wait()
 
 
 def fused(n, queries, keys, values, feature_weight, norm_gain, doc_bounds, out_grad):
@@ -524,24 +601,26 @@
     vm = pltpu.VMEM
     per = (heads, tokens, HS)
     slabs = (n, rows_each, HS)
-    scratch = [
+    whole = vm((tokens, features), bf)
+    scratch = [whole] * 8 + [
         vm((heads, HS), f32), vm((slab_rows, HS), bf), vm((slab_rows, HS), bf),
         vm((n, slab_rows, HS), bf), vm((heads, HS, HS), bf),
         vm((blocks, heads, HS, HS), f32),
         vm(slabs, bf), vm(slabs, bf), vm(slabs, bf), vm(slabs, bf),
-        vm(per, bf), vm(per, bf), vm(per, bf), vm(per, f32),
-        vm((blocks, heads, HS, HS), bf), vm(per, bf), vm((blocks, heads, HS, HS), f32),
+        vm(per, bf), vm(per, bf), vm(per, bf),
+        vm((heads, HS, blocks * HS), bf), vm(per, bf), vm((blocks, heads, HS, HS), f32),
         vm(slabs, bf), vm(slabs, bf), vm(slabs, bf), vm(slabs, bf),
-        vm(per, bf), vm((tokens, HS), bf), vm((tokens, HS), bf), vm(per, f32), vm(per, f32),
+        vm(per, bf), vm(per, bf), vm(per, f32), vm(per, f32),
         vm((heads, HS, HS), f32),
         vm((groups, n, slab_rows // groups, HS), bf), vm((groups, n, slab_rows // groups, HS), bf),
         vm((heads, HS), f32), vm((n, heads, HS), f32),
         vm((slab_rows, HS), f32), vm((slab_rows, HS), f32),
     ]
     dma = pltpu.SemaphoreType.DMA
-    sems = [dma, dma] + [dma((n,))] * 12 + [dma((groups, n))] * 2 + [dma, dma]
+    sems = [dma, dma] + [dma((n,))] * 12 + [dma((groups, n))] * 2 + [dma, dma, dma((8,))]
     flat = jax.ShapeDtypeStruct((tokens, features), bf)
     in_vmem = pl.BlockSpec(memory_space=vm)
+    anywhere = pl.BlockSpec(memory_space=pl.ANY)
     mixed, qgrad, kgrad, vgrad, wout, gout = pl.pallas_call(
         functools.partial(layer_kernel, n, heads, blocks, doc_bounds.shape[0], factor),
         out_shape=(
@@ -549,8 +628,8 @@
             jax.ShapeDtypeStruct((2, slab_rows, HS), f32),
             jax.ShapeDtypeStruct((heads, HS), f32),
         ),
-        in_specs=[pl.BlockSpec(memory_space=pltpu.SMEM)] + [in_vmem] * 6,
-        out_specs=(in_vmem,) * 6,
+        in_specs=[pl.BlockSpec(memory_space=pltpu.SMEM)] + [anywhere] * 4 + [in_vmem] * 2,
+        out_specs=(anywhere,) * 4 + (in_vmem,) * 2,
         scratch_shapes=scratch + sems,
         compiler_params=pltpu.CompilerParams(
             collective_id=0, has_side_effects=True, vmem_limit_bytes=52 * 2**20
@@ -561,6 +640,15 @@
         ),
         name="layer",
     )(doc_bounds, queries, keys, values, out_grad, norm_gain, wx)
+    mixed, qgrad, kgrad, vgrad = pl.pallas_call(
+        hand_on,
+        out_shape=(flat,) * 4,
+        in_specs=[anywhere] * 4,
+        out_specs=(anywhere,) * 4,
+        scratch_shapes=[dma((4,))],
+        compiler_params=pltpu.CompilerParams(vmem_limit_bytes=62 * 2**20),
+        name="hand_on",
+    )(mixed, qgrad, kgrad, vgrad)
     owned = wout.reshape(2 * heads, width, HS)
     owned = lax.dynamic_slice_in_dim(owned, lax.axis_index("fsdp") * deep, deep, 2)
     return mixed, qgrad, kgrad, vgrad, jnp.swapaxes(owned, 1, 2), gout

time: 78.8 us -> 190 us (2.41)
  Pallas kernels: 69.1 us -> 185 us
  local copies, waits for them, and re-layouts: 7.77 us -> 2.97 us
    pallas_call x0 -> x1, Pallas kernels: none -> 128 us  [fused(): pl.pallas_call(hand_on, out_shape=(flat,) * 4, in_specs=[anywhere] * 4, o...]
    pallas_call x1, Pallas kernels: 69.1 us -> 57 us  [fused(): pl.pallas_call(functools.partial(layer_kernel, n, heads, blocks, doc_boun...]
    unnamed x16 -> x8, local copies, waits for them, and re-layouts: 7.05 us -> 2.25 us
where the time goes in v2:
time: 190 us
  Pallas kernels  185 us (97%)
  local copies, waits for them, and re-layouts  2.97 us (2%)
    pallas_call x1, Pallas kernels, fused(): pl.pallas_call(hand_on, out_shape=(flat,) * 4, in_specs=[anywhere] * 4, o...  128 us
    pallas_call x1, Pallas kernels, fused(): pl.pallas_call(functools.partial(layer_kernel, n, heads, blocks, doc_boun...  57 us

profile of v2, /device:TPU:0, one launch (start us, length us, event | category | flops | bytes accessed | tf_op | source)
XLA Modules:
  0.0 189.8 jit_solution(17648998329290168038)
XLA Ops:
  0.6 0.0 copy-start.2
  0.6 0.9 pad_maximum_fusion.wx
  1.6 0.0 copy-done.2
  1.6 0.0 copy-start.1
  1.6 0.1 copy.13.bounds
  1.7 0.6 copy-done.1
  2.3 57.0 %layer.1 = (bf16[512,1024]{1,0:T(8,128)(2,1)S(1)}, bf16[512,1024]{1,0:T(8,128)(2,1)}, bf16[512,1024]{1,0:T(8,128)(2,1)}, bf16[512,1024]{1,0:T(8,128)(2,1)}, f32[...) custom-call(s32[4,2]{1,0:T(4,128)S(1)} %copy.13.bounds, bf16[512,1024]{1,0:T(8,128)(2,1)} %q_in.1, bf16[512,1024]{1,0:T(8,128)(2,1)} %k_in.1, ...), custom_call_target="tpu_custom_call" | custom-call | flops 2415919104 | bytes 8388608 | tf_op jit(solution)/shard_map/layer/pallas_call | solution.py:624
  59.3 0.0 copy-start
  59.3 1.0 copy-done
  60.2 128.2 %hand_on.1 = (bf16[512,1024]{1,0:T(8,128)(2,1)}, bf16[512,1024]{1,0:T(8,128)(2,1)}, bf16[512,1024]{1,0:T(8,128)(2,1)}, bf16[512,1024]{1,0:T(8,128)(2,1)}) custom-call(bf16[512,1024]{1,0:T(8,128)(2,1)} %copy-done, bf16[512,1024]{1,0:T(8,128)(2,1)} %get-tuple-element.17.refs_1_, bf16[512,1024]{1,0:T(8,128)(2,1)} %get-tuple-element.18.refs_2_, ...), custom_call_target="tpu_custom_call" | custom-call | tf_op jit(solution)/shard_map/hand_on/pallas_call | solution.py:643
  188.5 0.7 dynamic-slice_bitcast_fusion
  189.2 0.6 copy.15
Async XLA Ops:
  0.6 0.9 copy-start.2
  1.6 0.7 copy-start.1
  59.3 1.0 copy-start

commit v3 on v2

--- a/solution.py
+++ b/solution.py
@@ -197,7 +197,7 @@
     gain_f, wslab, wpart, gw, wt, mloc, mtot, rx, tx, back,
     qf, kf, prob, sh, dh, eloc, etot, rx2, tx2, back2,
     dotq, dqf, dkp, vgp, wgt, wgs, rwg, gl, gp, fin, rfin,
-    w_s, w_r, g_s, g_r, m_s, m_r, b_s, b_r, e_s, e_r, c_s, c_r, p_s, p_r, t_s, t_r, f_s, f_r, io,
+    w_s, w_r, g_s, g_r, h_s, m_s, m_r, b_s, b_r, e_s, e_r, c_s, c_r, p_s, p_r, t_s, t_r, f_s, f_r, io,
 ):
     me = lax.axis_index("seq")
     mine = lax.axis_index("fsdp")
@@ -265,8 +265,8 @@
 
     gain_f[...] = gain[...].astype(jnp.float32)
 
-    def outer_products(pair, carry):
-        heads_here = (2 * pair, 2 * pair + 1)
+    def outer_products(quad, carry):
+        heads_here = [4 * quad + j for j in range(4)]
         terms = [
             [tn(k[rows(b), columns(h)], v[rows(b), columns(h)]) for b in range(blocks)]
             for h in heads_here
@@ -284,7 +284,7 @@
 
     loads[0].wait()
     loads[1].wait()
-    lax.fori_loop(0, heads // 2, outer_products, 0)
+    lax.fori_loop(0, heads // 4, outer_products, 0)
     pl.semaphore_wait(barrier, n)
 
     weight_swap = pltpu.make_async_remote_copy(
@@ -307,12 +307,22 @@
     ).astype(jnp.bfloat16)
 
     def send_weights(step, carry):
-        p = lax.rem(me + step, n)
+        p = lax.rem(me + 2 * step, n)
         push(wslab, gw.at[me], g_s.at[p], g_r.at[me], p).start()
         return carry
 
-    lax.fori_loop(1, n, send_weights, 0)
+    sibling = me + 1 - 2 * lax.rem(me, 2)
+    lax.fori_loop(1, n // 2, send_weights, 0)
     gw[me] = wslab[...]
+    push(gw.at[me], gw.at[me], h_s.at[me], g_r.at[me], sibling).start()
+
+    def forward_weights(step, carry):
+        p = lax.rem(me + n - 2 * step, n)
+        push(wslab, gw.at[p], g_s.at[p], g_r.at[p], p).wait_recv()
+        push(gw.at[p], gw.at[p], h_s.at[p], g_r.at[p], sibling).start()
+        return carry
+
+    lax.fori_loop(1, n // 2, forward_weights, 0)
 
     def scan(total, arrived, parts, entered, in_s, in_r, out_s, out_r, backward):
         arrived[me] = total[me]
@@ -350,11 +360,11 @@
     scan(mtot, rx, tx, back, m_s, m_r, b_s, b_r, False)
 
     def await_weights(step, carry):
-        p = lax.rem(me + n - step, n)
-        push(wslab, gw.at[p], g_s.at[p], g_r.at[p], p).wait_recv()
-        return carry
-
-    lax.fori_loop(1, n, await_weights, 0)
+        p = lax.rem(sibling + n - 2 * step, n)
+        push(gw.at[p], gw.at[p], h_s.at[p], g_r.at[p], sibling).wait_recv()
+        return carry
+
+    lax.fori_loop(0, n // 2, await_weights, 0)
     causal = lax.broadcasted_iota(jnp.int32, (BLK, BLK), 0) >= lax.broadcasted_iota(
         jnp.int32, (BLK, BLK), 1
     )
@@ -451,9 +461,8 @@
     lax.fori_loop(1, n, send_gain, 0)
     gp[me] = gl[...]
 
-    def query_side(pair, carry):
-        heads_here = (2 * pair, 2 * pair + 1)
-        for h in heads_here:
+    def query_side(quad, carry):
+        for h in [4 * quad + j for j in range(4)]:
             scores = []
             for b in range(blocks):
                 score = nt(dh[h, rows(b), :], v[rows(b), columns(h)])
@@ -465,11 +474,11 @@
                 ).astype(jnp.bfloat16)
         return carry
 
-    lax.fori_loop(0, heads // 2, query_side, 0)
+    lax.fori_loop(0, heads // 4, query_side, 0)
     scan(etot, rx2, tx2, back2, e_s, e_r, c_s, c_r, True)
 
-    def local_terms(pair, carry):
-        for h in (2 * pair, 2 * pair + 1):
+    def local_terms(quad, carry):
+        for h in [4 * quad + j for j in range(4)]:
             grads = dqf[h]
             qgrad[:, columns(h)] = nn(grads, wt[h]).astype(jnp.bfloat16)
             wgt[h] = tn(grads, q[:, columns(h)])
@@ -478,7 +487,7 @@
                 vgp[h, rows(b), :] = tn(prob[h, rows(b), :], dh[h, rows(b), :])
         return carry
 
-    lax.fori_loop(0, heads // 2, local_terms, 0)
+    lax.fori_loop(0, heads // 4, local_terms, 0)
     stores[1].start()
 
     def key_pair_grads(pair):
@@ -559,7 +568,6 @@
     def sent(step, carry):
         p = lax.rem(me + step, n)
         push(mtot.at[p], rx.at[me], m_s.at[p], m_r.at[me], p).wait_send()
-        push(wslab, gw.at[me], g_s.at[p], g_r.at[me], p).wait_send()
         push(tx.at[p], back.at[me], b_s.at[p], b_r.at[me], p).wait_send()
         push(etot.at[p], rx2.at[me], e_s.at[p], e_r.at[me], p).wait_send()
         push(tx2.at[p], back2.at[me], c_s.at[p], c_r.at[me], p).wait_send()
@@ -571,18 +579,42 @@
         return carry
 
     lax.fori_loop(1, n, sent, 0)
+
+    def sent_weights(step, carry):
+        p = lax.rem(me + 2 * step, n)
+
+        @pl.when(step > 0)
+        def _():
+            push(wslab, gw.at[me], g_s.at[p], g_r.at[me], p).wait_send()
+
+        push(gw.at[p], gw.at[p], h_s.at[p], g_r.at[p], sibling).wait_send()
+        return carry
+
+    lax.fori_loop(0, n // 2, sent_weights, 0)
     for store in stores:
         store.wait()
     owned_swap.wait()
     wout[partner] = rfin[...]
 
 
-def hand_on(*refs):
-    copies = [pltpu.make_async_copy(refs[i], refs[4 + i], refs[8].at[i]) for i in range(4)]
-    for copy in copies:
-        copy.start()
-    for copy in copies:
-        copy.wait()
+def hand_on(mixed, qgrad, kgrad, vgrad, gains, *refs):
+    outs, held, sems = refs[:5], refs[5], refs[6]
+    half = mixed.shape[0] // 2
+    loads, stores = [], []
+    for i, array in enumerate((mixed, qgrad, kgrad, vgrad)):
+        for j in range(2):
+            at = pl.ds(j * half, half)
+            stop = held.at[i, at, :]
+            loads.append(pltpu.make_async_copy(array.at[at, :], stop, sems.at[0, i, j]))
+            stores.append(pltpu.make_async_copy(stop, outs[i].at[at, :], sems.at[1, i, j]))
+    for load in loads:
+        load.start()
+    outs[4][...] = gains[...]
+    for load, store in zip(loads, stores):
+        load.wait()
+        store.start()
+    for store in stores:
+        store.wait()
 
 
 def fused(n, queries, keys, values, feature_weight, norm_gain, doc_bounds, out_grad):
@@ -617,7 +649,7 @@
         vm((slab_rows, HS), f32), vm((slab_rows, HS), f32),
     ]
     dma = pltpu.SemaphoreType.DMA
-    sems = [dma, dma] + [dma((n,))] * 12 + [dma((groups, n))] * 2 + [dma, dma, dma((8,))]
+    sems = [dma, dma] + [dma((n,))] * 13 + [dma((groups, n))] * 2 + [dma, dma, dma((8,))]
     flat = jax.ShapeDtypeStruct((tokens, features), bf)
     in_vmem = pl.BlockSpec(memory_space=vm)
     anywhere = pl.BlockSpec(memory_space=pl.ANY)
@@ -632,7 +664,7 @@
         out_specs=(anywhere,) * 4 + (in_vmem,) * 2,
         scratch_shapes=scratch + sems,
         compiler_params=pltpu.CompilerParams(
-            collective_id=0, has_side_effects=True, vmem_limit_bytes=52 * 2**20
+            collective_id=0, has_side_effects=True, vmem_limit_bytes=58 * 2**20
         ),
         cost_estimate=pl.CostEstimate(
             flops=36 * tokens * features * HS, bytes_accessed=16 * tokens * features,
@@ -640,15 +672,15 @@
         ),
         name="layer",
     )(doc_bounds, queries, keys, values, out_grad, norm_gain, wx)
-    mixed, qgrad, kgrad, vgrad = pl.pallas_call(
+    mixed, qgrad, kgrad, vgrad, gout = pl.pallas_call(
         hand_on,
-        out_shape=(flat,) * 4,
-        in_specs=[anywhere] * 4,
-        out_specs=(anywhere,) * 4,
-        scratch_shapes=[dma((4,))],
-        compiler_params=pltpu.CompilerParams(vmem_limit_bytes=62 * 2**20),
+        out_shape=(flat,) * 4 + (jax.ShapeDtypeStruct((heads, HS), f32),),
+        in_specs=[anywhere] * 4 + [in_vmem],
+        out_specs=(anywhere,) * 4 + (in_vmem,),
+        scratch_shapes=[vm((4, tokens, features), bf), dma((2, 4, 2))],
+        compiler_params=pltpu.CompilerParams(vmem_limit_bytes=60 * 2**20),
         name="hand_on",
-    )(mixed, qgrad, kgrad, vgrad)
+    )(mixed, qgrad, kgrad, vgrad, gout)
     owned = wout.reshape(2 * heads, width, HS)
     owned = lax.dynamic_slice_in_dim(owned, lax.axis_index("fsdp") * deep, deep, 2)
     return mixed, qgrad, kgrad, vgrad, jnp.swapaxes(owned, 1, 2), gout

time: 190 us -> 62.3 us (0.33)
  Pallas kernels: 185 us -> 58.4 us
    pallas_call x1, Pallas kernels: 128 us -> 4.87 us  [fused(): pl.pallas_call(hand_on, out_shape=(flat,) * 4 + (jax.ShapeDtypeStruct((he...]
    pallas_call x1, Pallas kernels: 57 us -> 53.5 us  [fused(): pl.pallas_call(functools.partial(layer_kernel, n, heads, blocks, doc_boun...]
where the time goes in v3:
time: 62.3 us; the launch traced here: 62 us
  Pallas kernels  58.4 us (94%)
  other arithmetic  1.53 us (2%)
  local copies, waits for them, and re-layouts  1.39 us (2%)
  between operations  0.68 us (1%)
    pallas_call x1, Pallas kernels, fused(): pl.pallas_call(functools.partial(layer_kernel, n, heads, blocks, doc_boun...  53.5 us
    pallas_call x1, Pallas kernels, fused(): pl.pallas_call(hand_on, out_shape=(flat,) * 4 + (jax.ShapeDtypeStruct((he...  4.87 us
    concatenate x1, other arithmetic, fused(): wx = jnp.concatenate([turned, turned], axis=2)  1.53 us

profile of v3, /device:TPU:0, one launch (start us, length us, event | category | flops | bytes accessed | tf_op | source)
XLA Modules:
  0.0 62.0 jit_solution(2499486836031518543)
XLA Ops:
  0.6 0.0 copy-start.1
  0.6 1.5 %pad_maximum_fusion.wx = bf16[2,64,128]{2,1,0:T(8,128)(2,1)} fusion(bf16[2,64,64]{2,1,0:T(8,128)(2,1)} %bitcast.7), kind=kLoop, calls=%fused_computation.1 | loop fusion | flops 65536 | bytes 49152 | tf_op jit(solution)/shard_map/concatenate | solution.py:630
  2.2 0.0 copy-done.1
  2.2 0.7 %copy.13.bounds = s32[4,2]{1,0:T(4,128)} copy(s32[4,2]{0,1:T(2,128)S(1)} %copy-done.1) | data formatting | bytes 64 | tf_op args[5]
  2.8 53.5 %layer.1 = (bf16[512,1024]{1,0:T(8,128)(2,1)}, bf16[512,1024]{1,0:T(8,128)(2,1)}, bf16[512,1024]{1,0:T(8,128)(2,1)}, bf16[512,1024]{1,0:T(8,128)(2,1)}, f32[2,64,128]{2,1,0:T(8,128)}, /*index=5*/f32[8,128]{1,0:T(8,128)}) custom-call(s32[4,2]{1,0:T(4,128)} %copy.13.bounds, bf16[512,1024]{1,0:T(8,128)(2,1)} %q_in.1, bf16[512,1024]{1,0:T(8,128)(2,1)} %k_in.1, ...), custom_call_target="tpu_custom_call" | custom-call | flops 2415919104 | bytes 8388608 | tf_op jit(solution)/shard_map/layer/pallas_call | solution.py:656
  56.4 0.0 copy-start
  56.4 4.9 %hand_on.1 = (bf16[512,1024]{1,0:T(8,128)(2,1)}, bf16[512,1024]{1,0:T(8,128)(2,1)}, bf16[512,1024]{1,0:T(8,128)(2,1)}, bf16[512,1024]{1,0:T(8,128)(2,1)}, f32[8,128]{1,0:T(8,128)}) custom-call(bf16[512,1024]{1,0:T(8,128)(2,1)} %get-tuple-element.17.mixed, bf16[512,1024]{1,0:T(8,128)(2,1)} %get-tuple-element.18.qgrad, ...), custom_call_target="tpu_custom_call" | custom-call | tf_op jit(solution)/shard_map/hand_on/pallas_call | solution.py:675
  61.3 0.0 copy-done
  61.3 0.7 %dynamic-slice_bitcast_fusion = f32[16,64,8]{1,2,0:T(8,128)} fusion(f32[16,8,128]{2,1,0:T(8,128)S(1)} %bitcast.6, s32[]{:T(128)S(6)} %select_n.3), kind=kLoop, calls=%fused_computation | loop fusion | bytes 65540 | tf_op jit(solution)/shard_map/transpose | solution.py:686
Async XLA Ops:
  0.6 1.5 %copy-start.1 = (s32[4,2]{0,1:T(2,128)S(1)}, s32[4,2]{0,1:T(2,128)}, u32[]{:S(2)}) copy-start(s32[4,2]{0,1:T(2,128)} %param.12) | copy-start | bytes 100
  56.4 4.9 %copy-start = (f32[2,64,128]{2,1,0:T(8,128)S(1)}, f32[2,64,128]{2,1,0:T(8,128)}, u32[]{:S(2)}) copy-start(f32[2,64,128]{2,1,0:T(8,128)} %get-tuple-element.26) | copy-start | bytes 196612
